TPU v7x, 32 devices: a whole 2x2x4 slice. The times are simulated.
32 devices in a mesh: lat: 8 (over z, x), deg: 4 (over y, core).
Axes of the slice: x: 2, y: 2, z: 4, core: 2. Of those that a mesh axis runs over, the one named last changes fastest.
Arguments:
- eta_tl: float32 [64, 10752], P('lat'), may hold values from -6 to 6
- vel_tl: float32 [2, 64, 10752], P(None, 'lat'), may hold values from -6 to 6
- eta_adj: float32 [64, 10752], P('lat'), may hold values from -6 to 6
- vel_adj: float32 [2, 64, 10752], P(None, 'lat'), may hold values from -6 to 6
- depth: float32 [64, 10752], P('lat'), may hold values from 0.2 to 1
- drag: float32 [64, 10752], P('lat'), may hold values from 0.01 to 0.3
- ocean: int32 [64, 10752], P('lat'), may hold values 0 or 1
- basis: bfloat16 [1024, 64, 1024], P('lat', None, 'deg'), may hold values from -5 to 5
- love: float32 [1024], P('deg'), may hold values from 0.05 to 0.5
Outputs:
- eta_tl_out: float32 [64, 10752], P('lat')
- vel_tl_out: float32 [2, 64, 10752], P(None, 'lat')
- eta_adj_out: float32 [64, 10752], P('lat')
- vel_adj_out: float32 [2, 64, 10752], P(None, 'lat')
All inputs are finite; a program needn't handle non-finite values. No bound on the sum of `ocean` on one device may be relied on, other than what follows from the above.
Results may differ from a plain program's by a relative error of at most 0.02.
Values may be sent and summed in bfloat16 or wider, within the bound.
A program may use at most 320 MiB of HBM per device.

v0:
```python
import jax
import jax.numpy as jnp
from jax import lax
from jax.sharding import PartitionSpec as P

STEPS = 2
kappa_x = 0.3
kappa_y = 0.4


def as_sent(value):
    return jax.tree.map(lambda a: a.astype(jnp.bfloat16) if a.dtype == jnp.float32 else a, value)


def passed_along(value, axis, by):
    length = lax.axis_size(axis)
    pairs = [(i, i + by) for i in range(length) if 0 <= i + by < length]
    return lax.ppermute(value, axis, pairs)


def trig_table(orders, lon_count):
    lon_cells = jnp.arange(lon_count, dtype=jnp.int32)
    phase_index = lon_cells[:, None] * orders[None, :] % lon_count
    angles = phase_index.astype(jnp.float32) * (2.0 * jnp.pi / lon_count)
    return jnp.concatenate([jnp.cos(angles), jnp.sin(angles)], axis=1).astype(jnp.bfloat16)


def order_factor(orders):
    return jnp.where(orders == 0, 1.0, 2.0).astype(jnp.bfloat16)


def analyse(stacked, analysis_weight, table_now, order_count):
    row_count = stacked.shape[1]
    lon_count = stacked.shape[2]
    flat_rows = stacked.astype(jnp.bfloat16).reshape(2 * row_count, lon_count)
    spectra = lax.dot_general(
        table_now, flat_rows, (((0,), (1,)), ((), ())), preferred_element_type=jnp.float32
    )
    spectra = spectra.reshape(2, order_count, 2, row_count) * (1.0 / lon_count)
    return (spectra * analysis_weight[None, None, :, :]).astype(jnp.bfloat16)


def legendre(spectra, basis, love):
    coeffs = jnp.einsum("cmfi,mil->cmfl", spectra, basis, preferred_element_type=jnp.float32)
    scaled = (coeffs * love[None, None, None, :]).astype(jnp.bfloat16)
    return jnp.einsum("cmfl,mil->cmfi", scaled, basis, preferred_element_type=jnp.float32)


def synthesise(coeffs, factors, table_now, output_weight):
    order_count = coeffs.shape[1]
    row_count = coeffs.shape[3]
    scaled = (coeffs * factors[None, :, None, None]).reshape(2 * order_count, 2 * row_count)
    grid_out = lax.dot_general(
        scaled, table_now, (((0,), (1,)), ((), ())), preferred_element_type=jnp.float32
    )
    return grid_out.reshape(2, row_count, -1) * output_weight[:, :, None]


def from_north(edge_row):
    return passed_along(as_sent(edge_row), "lat", -1).astype(edge_row.dtype)


def from_south(edge_row):
    return passed_along(as_sent(edge_row), "lat", 1).astype(edge_row.dtype)


def on_device(eta_tl, vel_tl, eta_adj, vel_adj, depth, drag, ocean, basis, love):
    row_count = eta_tl.shape[0]
    lon_count = eta_tl.shape[1]
    lat_count = lax.axis_size("lat")
    total_rows = row_count * lat_count
    first_row = lax.axis_index("lat") * row_count
    indices = first_row + jnp.arange(row_count, dtype=jnp.int32)
    latitude = (indices.astype(jnp.float32) + 0.5) * (jnp.pi / total_rows) - 0.5 * jnp.pi
    cosine = jnp.cos(latitude)
    quad_weight = jnp.pi / total_rows * cosine
    east_factor = (kappa_x / (0.5 + 0.5 * cosine))[:, None]
    wet_mask = ocean.astype(jnp.float32)
    north_depth, north_wet = (
        passed_along(depth[:1].astype(jnp.bfloat16), "lat", -1).astype(jnp.float32),
        passed_along(wet_mask[:1].astype(jnp.bfloat16), "lat", -1).astype(jnp.float32),
    )
    depth_up = jnp.concatenate([depth[1:], north_depth], 0)
    wet_up = jnp.concatenate([wet_mask[1:], north_wet], 0)
    mask_u = wet_mask * jnp.roll(wet_mask, -1, 1)
    mask_v = wet_mask * wet_up
    depth_u = 0.5 * (depth + jnp.roll(depth, -1, 1))
    depth_v = 0.5 * (depth + depth_up)
    retain = 1.0 - drag
    ones_weight = jnp.ones_like(quad_weight)
    analysis_weight = jnp.stack([quad_weight, ones_weight])
    output_weight = jnp.stack([ones_weight, quad_weight])
    owned_count = basis.shape[0]
    order_total = owned_count * lat_count
    full_orders = jnp.arange(order_total, dtype=jnp.int32)
    full_table = trig_table(full_orders, lon_count)
    full_factor = order_factor(full_orders)
    state_eta, state_vel = (eta_tl, vel_tl)
    back_eta, back_vel = (eta_adj, vel_adj)
    for step_index in range(STEPS):
        flux_east = east_factor * wet_mask * back_eta
        flux_north = kappa_y * wet_mask * back_eta
        north_up = jnp.concatenate([flux_north[1:], from_north(flux_north[:1])], 0)
        p_term = mask_u * (back_vel[0] + depth_u * (jnp.roll(flux_east, -1, 1) - flux_east))
        q_term = mask_v * (back_vel[1] + depth_v * (north_up - flux_north))
        q_down = jnp.concatenate([from_south(q_term[-1:]), q_term[:-1]], 0)
        flux_p = east_factor * p_term
        psi_bar = flux_p - jnp.roll(flux_p, 1, 1) + kappa_y * (q_term - q_down)
        spectra = analyse(jnp.stack([state_eta, psi_bar]), analysis_weight, full_table, order_total)
        owned_rows = lax.all_to_all(spectra, "lat", split_axis=1, concat_axis=3, tiled=True)
        partial_value = legendre(owned_rows, basis, love)
        total_sum = lax.psum(partial_value.astype(jnp.bfloat16), "deg")
        banded = lax.all_to_all(total_sum, "lat", split_axis=3, concat_axis=1, tiled=True)
        loads = synthesise(banded, full_factor, full_table, output_weight)
        psi_now = state_eta - loads[0]
        psi_up = jnp.concatenate([psi_now[1:], from_north(psi_now[:1])], 0)
        new_u = mask_u * (
            retain * state_vel[0] - east_factor * (jnp.roll(psi_now, -1, 1) - psi_now)
        )
        new_v = mask_v * (retain * state_vel[1] - kappa_y * (psi_up - psi_now))
        flux_x = depth_u * new_u
        flux_y = depth_v * new_v
        flux_down = jnp.concatenate([from_south(flux_y[-1:]), flux_y[:-1]], 0)
        state_eta = state_eta - wet_mask * (
            east_factor * (flux_x - jnp.roll(flux_x, 1, 1)) + kappa_y * (flux_y - flux_down)
        )
        state_vel = jnp.stack([new_u, new_v])
        back_eta = back_eta + psi_bar - loads[1]
        back_vel = jnp.stack([retain * p_term, retain * q_term])
    return (state_eta, state_vel, back_eta, back_vel)


def solution(mesh):
    in_specs = (
        P("lat", None),
        P(None, "lat", None),
        P("lat", None),
        P(None, "lat", None),
        P("lat", None),
        P("lat", None),
        P("lat", None),
        P("lat", None, "deg"),
        P("deg"),
    )
    out_specs = (P("lat", None), P(None, "lat", None), P("lat", None), P(None, "lat", None))
    return jax.shard_map(
        on_device, mesh=mesh, in_specs=in_specs, out_specs=out_specs, check_vma=False
    )
```

profile of v0, /device:TPU:0, one launch (start us, length us, event | category | flops | bytes accessed | tf_op | source)
XLA Modules:
  0.0 552.0 jit_solution(11705418563088993422)
XLA Ops:
  14.5 187.3 %sine_convert_fusion = (bf16[10752,1024]{1,0:T(8,128)(2,1)}, bf16[10752,1024]{1,0:T(8,128)(2,1)}) fusion(), kind=kLoop, calls=%fused_computation.8 | loop fusion | flops 121110528 | bytes 44040192 | tf_op jit(solution)/shard_map/convert.19
  202.5 29.5 %fusion.9 = bf16[2048,10752]{0,1:T(8,128)(2,1)} fusion(bf16[10752,1024]{1,0:T(8,128)(2,1)} %get-tuple-element.48, bf16[10752,1024]{1,0:T(8,128)(2,1)} %get-tuple-element.49), kind=kLoop, calls=%fused_computation.14 | loop fusion | flops 88080384 | bytes 88080384 | tf_op jit(solution)/shard_map/dot_general | solution.py:36
  232.9 2.4 broadcast_multiply_fusion.1
  235.3 6.7 %collective-permute-start.3 = (bf16[1,10752]{1,0:T(2,128)(2,1)S(1)}, bf16[1,10752]{1,0:T(2,128)(2,1)S(1)}, u32[]{:S(2)}, u32[]{:S(2)}) collective-permute-start(bf16[1,10752]{1,0:T(2,128)(2,1)S(1)} %slice.279), channel_id=1, source_target_pairs={{0,4},{4,8},{8,12},{12,16},{16,20},{20,24},{24,28},{1,5},{5,9},{9,... | collective-permute-start | bytes 64520 | tf_op jit(solution)/shard_map/ppermute | solution.py:18
  242.1 56.8 %copy.41 = bf16[2048,10752]{1,0:T(8,128)(2,1)} copy(bf16[2048,10752]{0,1:T(8,128)(2,1)} %fusion.9) | data formatting | bytes 88080384 | tf_op jit(solution)/shard_map/dot_general | solution.py:36
  299.9 19.5 %fusion.66 = bf16[2,1024,2,8]{1,3,2,0:T(8,128)(2,1)S(1)} fusion(bf16[2,1024,10752,1]{2,1,3,0:T(8,128)(2,1)} %bitcast.190, bf16[1,8,10752]{2,1,0:T(8,128)(2,1)S(1)} %get-tuple-element.22, bf16[1,8,10752]{2,1,0:T(8,128)(2,1)S(1)} %copy-done.10, f32[2,8]{1,0:T(2,128)S(1)} %get-tuple-element.46), kind=kOutput, calls=%fused_computation.37 | convolution fusion | flops 705396736 | bytes 44449856 | tf_op jit(solution)/shard_map/dot_general | solution.py:36
  321.2 14.8 %all_to_all.72 = bf16[8,2,2048]{2,1,0:T(2,128)(2,1)S(1)} all-to-all(bf16[8,2,2048]{2,1,0:T(2,128)(2,1)S(1)} %reshape.79), channel_id=1, replica_groups=mesh['lat'=8,'deg'=4] {'lat'}, dimensions={0} | all-to-all | bytes 131072 | tf_op jit(solution)/shard_map/all_to_all | solution.py:110
  337.2 1.3 copy.59
  338.6 6.0 %fusion.61 = bf16[2,128,2,64]{3,2,0,1:T(2,128)(2,1)} fusion(bf16[128,64,256]{2,1,0:T(8,128)(2,1)} %param.16, bf16[2,128,2,64]{3,2,0,1:T(2,128)(2,1)S(1)} %copy.45, f32[256]{0:T(256)S(1)} %copy-done.11), kind=kOutput, calls=%fused_computation.34 | convolution fusion | flops 33849344 | bytes 4326400 | tf_op jit(solution)/shard_map/cmfl,mil->cmfi/dot_general | solution.py:46
  344.7 29.1 %all-reduce.5.cloned.1.call-done = bf16[2,128,2,64]{3,2,0,1:T(2,128)(2,1)} async-done(((bf16[2,128,2,64]{3,2,0,1:T(2,128)(2,1)}), bf16[2,128,2,64]{3,2,0,1:T(2,128)(2,1)}) %all-reduce.5.cloned.1.call-update) | async-done | bytes 65552 | tf_op jit(solution)/shard_map/psum | solution.py:112
  373.8 1.7 copy.46
  375.5 5.5 all-to-all-start.1
  381.1 6.8 %all-to-all-done.1 = bf16[2,128,2,64]{1,2,0,3:T(2,128)(2,1)S(1)} async-done(((bf16[2,128,2,64]{1,2,0,3:T(2,128)(2,1)}), bf16[2,128,2,64]{1,2,0,3:T(2,128)(2,1)S(1)}, u32[]{:S(2)}, u32[]{:S(2)}) %all-to-all-start.1) | async-done | bytes 65568 | tf_op jit(solution)/shard_map/all_to_all | solution.py:113
  388.0 18.4 %fusion.10 = f32[2,8,10752]{2,1,0:T(8,128)} fusion(bf16[10752,1024]{1,0:T(8,128)(2,1)} %get-tuple-element.48, bf16[10752,1024]{1,0:T(8,128)(2,1)} %get-tuple-element.49, f32[2,8]{1,0:T(2,128)S(1)} %get-tuple-element.47, bf16[2048,16]{0,1:T(8,128)(2,1)S(1)} %all_to_all.59, bf16[2048]{0:T(1024)(128)(2,1)S(1)} %bitcast.210), kind=kOutput, calls=%fused_computation.15 | convolution fusion | flops 792928256 | bytes 44798016 | tf_op jit(solution)/shard_map/dot_general | solution.py:53
  406.4 1.4 multiply_multiply_fusion
  410.7 3.0 collective-permute-done.4
  413.8 1.9 collective-permute-done.6
  415.8 2.4 fusion.139
  418.2 4.8 collective-permute-start.5
  423.2 2.3 collective-permute-start.7
  425.9 1.8 multiply_bitcast_fusion.1
  428.2 19.5 %fusion.67 = bf16[2,1024,2,8]{1,3,2,0:T(8,128)(2,1)S(1)} fusion(bf16[2,1024,10752,1]{2,1,3,0:T(8,128)(2,1)} %bitcast.191, bf16[1,8,10752]{2,1,0:T(8,128)(2,1)S(1)} %get-tuple-element.14, bf16[1,8,10752]{2,1,0:T(8,128)(2,1)S(1)} %get-tuple-element.12, f32[2,8]{1,0:T(2,128)S(1)} %get-tuple-element.46), kind=kOutput, calls=%fused_computation.38 | convolution fusion | flops 705396736 | bytes 44449856 | tf_op jit(solution)/shard_map/dot_general | solution.py:36
  449.5 10.5 %all_to_all.73 = bf16[8,2,2048]{2,1,0:T(2,128)(2,1)S(1)} all-to-all(bf16[8,2,2048]{2,1,0:T(2,128)(2,1)S(1)} %reshape.81), channel_id=1, replica_groups=mesh['lat'=8,'deg'=4] {'lat'}, dimensions={0} | all-to-all | bytes 131072 | tf_op jit(solution)/shard_map/all_to_all | solution.py:110
  463.3 6.1 %fusion.56 = bf16[2,128,2,64]{3,2,0,1:T(2,128)(2,1)} fusion(bf16[128,64,256]{2,1,0:T(8,128)(2,1)} %param.16, bf16[2,128,2,64]{3,2,0,1:T(2,128)(2,1)} %copy.52, f32[256]{0:T(256)S(1)} %copy-done.11), kind=kOutput, calls=%fused_computation.33 | convolution fusion | flops 33849344 | bytes 4326400 | tf_op jit(solution)/shard_map/cmfl,mil->cmfi/dot_general | solution.py:46
  469.4 28.1 %all-reduce.7.cloned.1.call-done = bf16[2,128,2,64]{3,2,0,1:T(2,128)(2,1)} async-done(((bf16[2,128,2,64]{3,2,0,1:T(2,128)(2,1)}), bf16[2,128,2,64]{3,2,0,1:T(2,128)(2,1)}) %all-reduce.7.cloned.1.call-update) | async-done | bytes 65552 | tf_op jit(solution)/shard_map/psum | solution.py:112
  498.6 12.2 %all_to_all.74 = bf16[2,128,2,64]{1,2,0,3:T(2,128)(2,1)S(1)} all-to-all(bf16[2,128,2,64]{1,2,0,3:T(2,128)(2,1)S(1)} %copy.53), channel_id=1, replica_groups=mesh['lat'=8,'deg'=4] {'lat'}, dimensions={3} | all-to-all | bytes 131072 | tf_op jit(solution)/shard_map/all_to_all | solution.py:113
  511.5 18.4 %fusion.13 = f32[2,8,10752]{2,1,0:T(8,128)} fusion(bf16[10752,1024]{1,0:T(8,128)(2,1)} %get-tuple-element.48, bf16[10752,1024]{1,0:T(8,128)(2,1)} %get-tuple-element.49, f32[2,8]{1,0:T(2,128)S(1)} %get-tuple-element.47, bf16[2048,16]{0,1:T(8,128)(2,1)} %all_to_all.67, bf16[2048]{0:T(1024)(128)(2,1)S(1)} %bitcast.211), kind=kOutput, calls=%fused_computation.16 | convolution fusion | flops 792928256 | bytes 44798016 | tf_op jit(solution)/shard_map/dot_general | solution.py:53
  529.9 1.9 fusion.68
  533.2 1.9 pad_maximum_fusion.4
  535.2 2.5 collective-permute-done.8
  537.8 1.4 fusion.130
  539.3 3.2 collective-permute-start.9
  (115 shorter events, 28.0 us)
Async XLA Ops:
  7.2 194.6 %copy-start.2 = (f32[8,10752]{1,0:T(8,128)S(1)}, f32[8,10752]{1,0:T(8,128)}, u32[]{:S(2)}) copy-start(f32[8,10752]{1,0:T(8,128)} %param.9) | copy-start | bytes 1032196
  7.2 366.7 %all-reduce.5.cloned.1.call-start = ((), (), s32[]{:S(2)}) async-start(), calls=%async_computation.4 | async-start | bytes 262144 | tf_op jit(solution)/shard_map/psum | solution.py:112
  8.5 224.2 %collective-permute-start.2 = (bf16[1,10752]{1,0:T(2,128)(2,1)S(1)}, bf16[1,10752]{1,0:T(2,128)(2,1)S(1)}, u32[]{:S(2)}, u32[]{:S(2)}) collective-permute-start(bf16[1,10752]{1,0:T(2,128)(2,1)S(1)} %slice.280), channel_id=1, source_target_pairs={{4,0},{8,4},{12,8},{16,12},{20,16},{24,20},{28,24},{5,1},{9,5},{13... | collective-permute-start | bytes 64520 | tf_op jit(solution)/shard_map/ppermute | solution.py:18
  10.8 221.9 %collective-permute-start.1 = (bf16[1,10752]{1,0:T(2,128)(2,1)S(1)}, bf16[1,10752]{1,0:T(2,128)(2,1)S(1)}, u32[]{:S(2)}, u32[]{:S(2)}) collective-permute-start(bf16[1,10752]{1,0:T(2,128)(2,1)S(1)} %slice.281), channel_id=1, source_target_pairs={{4,0},{8,4},{12,8},{16,12},{20,16},{24,20},{28,24},{5,1},{9,5},{13... | collective-permute-start | bytes 64520 | tf_op jit(solution)/shard_map/ppermute | solution.py:18
  13.2 219.7 %collective-permute-start = (bf16[1,10752]{1,0:T(2,128)(2,1)S(1)}, bf16[1,10752]{1,0:T(2,128)(2,1)S(1)}, u32[]{:S(2)}, u32[]{:S(2)}) collective-permute-start(bf16[1,10752]{1,0:T(2,128)(2,1)S(1)} %slice.282), channel_id=1, source_target_pairs={{4,0},{8,4},{12,8},{16,12},{20,16},{24,20},{28,24},{5,1},{9,5},{13... | collective-permute-start | bytes 64520 | tf_op jit(solution)/shard_map/ppermute | solution.py:18
  202.5 29.9 %copy-start.1 = (f32[8,10752]{1,0:T(8,128)S(1)}, f32[8,10752]{1,0:T(8,128)}, u32[]{:S(2)}) copy-start(f32[8,10752]{1,0:T(8,128)} %param.13) | copy-start | bytes 1032196
  202.5 30.4 %copy-start = (s32[8,10752]{1,0:T(8,128)S(1)}, s32[8,10752]{1,0:T(8,128)}, u32[]{:S(2)}) copy-start(s32[8,10752]{1,0:T(8,128)} %param.15) | copy-start | bytes 1032196
  202.5 30.4 %slice-start = ((f32[8,10752]{1,0:T(8,128)}), f32[8,1]{1,0:T(8,128)S(1)}, s32[]{:S(2)}) async-start(f32[8,10752]{1,0:T(8,128)} %param.13), calls=%async_computation.6 | async-start | bytes 8192 | tf_op jit(solution)/shard_map/jit(_roll_static)/slice | solution.py:87
  235.2 180.5 %copy-start.5 = (f32[8,10752]{1,0:T(8,128)}, f32[8,10752]{1,0:T(8,128)S(1)}, u32[]{:S(2)}) copy-start(f32[8,10752]{1,0:T(8,128)S(1)} %get-tuple-element.34) | copy-start | bytes 1032196
  235.3 63.6 %collective-permute-start.3 = (bf16[1,10752]{1,0:T(2,128)(2,1)S(1)}, bf16[1,10752]{1,0:T(2,128)(2,1)S(1)}, u32[]{:S(2)}, u32[]{:S(2)}) collective-permute-start(bf16[1,10752]{1,0:T(2,128)(2,1)S(1)} %slice.279), channel_id=1, source_target_pairs={{0,4},{4,8},{8,12},{12,16},{16,20},{20,24},{24,28},{1,5},{5,9},{9,... | collective-permute-start | bytes 64520 | tf_op jit(solution)/shard_map/ppermute | solution.py:18
  242.0 57.8 %copy-start.10 = (bf16[1,8,10752]{2,1,0:T(8,128)(2,1)S(1)}, bf16[1,8,10752]{2,1,0:T(8,128)(2,1)}, u32[]{:S(2)}) copy-start(bf16[1,8,10752]{2,1,0:T(8,128)(2,1)} %convert_bitcast_fusion.3) | copy-start | bytes 516100
  298.8 39.8 %copy-start.11 = (f32[256]{0:T(256)S(1)}, f32[256]{0:T(256)}, u32[]{:S(2)}) copy-start(f32[256]{0:T(256)} %param.17) | copy-start | bytes 3076
  338.6 77.2 %copy-start.3 = (f32[8,10752]{1,0:T(8,128)S(1)}, f32[8,10752]{1,0:T(8,128)}, u32[]{:S(2)}) copy-start(f32[8,10752]{1,0:T(8,128)} %param.14) | copy-start | bytes 1032196
  338.6 77.2 %copy-start.7 = (f32[8,10752]{1,0:T(8,128)S(1)}, f32[8,10752]{1,0:T(8,128)}, u32[]{:S(2)}) copy-start(f32[8,10752]{1,0:T(8,128)} %get-tuple-element.35) | copy-start | bytes 1032196
  375.5 12.4 %all-to-all-start.1 = ((bf16[2,128,2,64]{1,2,0,3:T(2,128)(2,1)}), bf16[2,128,2,64]{1,2,0,3:T(2,128)(2,1)S(1)}, u32[]{:S(2)}, u32[]{:S(2)}) async-start(bf16[2,128,2,64]{1,2,0,3:T(2,128)(2,1)} %copy.46), calls=%async_computation.1 | async-start | bytes 131072 | tf_op jit(solution)/shard_map/all_to_all | solution.py:113
  381.0 116.6 %all-reduce.7.cloned.1.call-start = ((), (), s32[]{:S(2)}) async-start(), calls=%async_computation.5 | async-start | bytes 262144 | tf_op jit(solution)/shard_map/psum | solution.py:112
  407.8 5.9 %collective-permute-start.4 = (bf16[1,10752]{1,0:T(2,128)(2,1)S(1)}, bf16[1,10752]{1,0:T(2,128)(2,1)S(1)}, u32[]{:S(2)}, u32[]{:S(2)}) collective-permute-start(bf16[1,10752]{1,0:T(2,128)(2,1)S(1)} %slice.278), channel_id=1, source_target_pairs={{4,0},{8,4},{12,8},{16,12},{20,16},{24,20},{28,24},{5,1},{9,5},{13... | collective-permute-start | bytes 64520 | tf_op jit(solution)/shard_map/ppermute | solution.py:18
  409.2 6.5 %collective-permute-start.6 = (bf16[1,10752]{1,0:T(2,128)(2,1)S(1)}, bf16[1,10752]{1,0:T(2,128)(2,1)S(1)}, u32[]{:S(2)}, u32[]{:S(2)}) collective-permute-start(bf16[1,10752]{1,0:T(2,128)(2,1)S(1)} %slice.276), channel_id=1, source_target_pairs={{4,0},{8,4},{12,8},{16,12},{20,16},{24,20},{28,24},{5,1},{9,5},{13... | collective-permute-start | bytes 64520 | tf_op jit(solution)/shard_map/ppermute | solution.py:18
  418.2 7.3 %collective-permute-start.5 = (bf16[1,10752]{1,0:T(2,128)(2,1)S(1)}, bf16[1,10752]{1,0:T(2,128)(2,1)S(1)}, u32[]{:S(2)}, u32[]{:S(2)}) collective-permute-start(bf16[1,10752]{1,0:T(2,128)(2,1)S(1)} %slice.277), channel_id=1, source_target_pairs={{0,4},{4,8},{8,12},{12,16},{16,20},{20,24},{24,28},{1,5},{5,9},{9,... | collective-permute-start | bytes 64520 | tf_op jit(solution)/shard_map/ppermute | solution.py:18
  423.2 4.8 collective-permute-start.7
  460.0 73.2 %copy-start.9 = (f32[1,8,10752]{2,1,0:T(8,128)S(1)}, f32[1,8,10752]{2,1,0:T(8,128)}, u32[]{:S(2)}) copy-start(f32[1,8,10752]{2,1,0:T(8,128)} %get-tuple-element.4) | copy-start | bytes 1032196
  463.3 74.5 %copy-start.4 = (f32[8,10752]{1,0:T(8,128)S(1)}, f32[8,10752]{1,0:T(8,128)}, u32[]{:S(2)}) copy-start(f32[8,10752]{1,0:T(8,128)} %param.14) | copy-start | bytes 1032196
  463.3 74.5 %copy-start.6 = (f32[8,10752]{1,0:T(8,128)S(1)}, f32[8,10752]{1,0:T(8,128)}, u32[]{:S(2)}) copy-start(f32[8,10752]{1,0:T(8,128)} %copy-done.5) | copy-start | bytes 1032196
  463.3 74.5 %copy-start.8 = (f32[8,10752]{1,0:T(8,128)S(1)}, f32[8,10752]{1,0:T(8,128)}, u32[]{:S(2)}) copy-start(f32[8,10752]{1,0:T(8,128)} %get-tuple-element.35) | copy-start | bytes 1032196
  531.9 5.9 %collective-permute-start.8 = (bf16[1,10752]{1,0:T(2,128)(2,1)S(1)}, bf16[1,10752]{1,0:T(2,128)(2,1)S(1)}, u32[]{:S(2)}, u32[]{:S(2)}) collective-permute-start(bf16[1,10752]{1,0:T(2,128)(2,1)S(1)} %slice.274), channel_id=1, source_target_pairs={{4,0},{8,4},{12,8},{16,12},{20,16},{24,20},{28,24},{5,1},{9,5},{13... | collective-permute-start | bytes 64520 | tf_op jit(solution)/shard_map/ppermute | solution.py:18
  539.3 4.9 collective-permute-start.9
Sparse Core Ops, SparseCore 0:
  344.8 28.9 all-reduce.4
  469.6 27.9 all-reduce.6
where the time goes:
time: 554 us; the launch traced here: 552 us
  other arithmetic  237 us (43%)
  matrix products  88 us (16%)
  local copies, waits for them, and re-layouts  72.5 us (13%)
  waiting for transfers between devices  72.3 us (13%)
  blocking collectives  37.5 us (7%)
  starting transfers between devices  30.4 us (5%)
  between operations  14.7 us (3%)
    another operation x1, other arithmetic  187 us
    psum x2, waiting for transfers between devices, on_device(): total_sum = lax.psum(partial_value.astype(jnp.bfloat16), 'deg')  57.2 us
    dot_general x1, local copies, waits for them, and re-layouts, analyse(): lax.dot_general(table_now, flat_rows, (((0,), (1,)), ((), ())), preferred...  56.8 us
    dot_general x2, matrix products, analyse(): lax.dot_general(table_now, flat_rows, (((0,), (1,)), ((), ())), preferred...  39 us
    dot_general x2, matrix products, synthesise(): lax.dot_general(scaled, table_now, (((0,), (1,)), ((), ())), preferred_el...  36.8 us
    dot_general x1, other arithmetic, analyse(): lax.dot_general(table_now, flat_rows, (((0,), (1,)), ((), ())), preferred...  29.5 us
    all_to_all x2, blocking collectives, on_device(): lax.all_to_all(spectra, 'lat', split_axis=1, concat_axis=3, tiled=True)  25.3 us
    ppermute x10, starting transfers between devices, passed_along(): return lax.ppermute(value, axis, pairs)  24.8 us
  transfers between devices with their start and end apart: 13, of which 7 were waited for; matrix products, arithmetic and copies ran while one was open for 51% of the time, Pallas kernels for 0%

commit v1 on v0

--- a/solution.py
+++ b/solution.py
@@ -109,7 +109,7 @@
         spectra = analyse(jnp.stack([state_eta, psi_bar]), analysis_weight, full_table, order_total)
         owned_rows = lax.all_to_all(spectra, "lat", split_axis=1, concat_axis=3, tiled=True)
         partial_value = legendre(owned_rows, basis, love)
-        total_sum = lax.psum(partial_value.astype(jnp.bfloat16), "deg")
+        total_sum = jnp.sum(lax.all_gather(partial_value.astype(jnp.bfloat16), "deg"), axis=0)
         banded = lax.all_to_all(total_sum, "lat", split_axis=3, concat_axis=1, tiled=True)
         loads = synthesise(banded, full_factor, full_table, output_weight)
         psi_now = state_eta - loads[0]

time: 554 us -> 491 us (0.89)
  waiting for transfers between devices: 72.3 us -> 21.9 us
  between operations: 14.7 us -> 1.29 us
  starting transfers between devices: 30.4 us -> 36.5 us
  local copies, waits for them, and re-layouts: 72.5 us -> 66.8 us
    psum x2 -> x0, waiting for transfers between devices: 57.2 us -> none  [on_device(): total_sum = lax.psum(partial_value.astype(jnp.bfloat16), 'deg')]
    all_to_all x2 -> x1, blocking collectives: 25.3 us -> 10.3 us  [on_device(): lax.all_to_all(spectra, 'lat', split_axis=1, concat_axis=3, tiled=True)]
    all_gather x0 -> x2, blocking collectives: none -> 15 us  [on_device(): lax.all_gather(partial_value.astype(jnp.bfloat16), 'deg')]
    all_to_all x0 -> x1, starting transfers between devices: none -> 8.1 us  [on_device(): lax.all_to_all(spectra, 'lat', split_axis=1, concat_axis=3, tiled=True)]
    all_to_all x0 -> x1, waiting for transfers between devices: none -> 6.9 us  [on_device(): lax.all_to_all(spectra, 'lat', split_axis=1, concat_axis=3, tiled=True)]
  transfers between devices with their start and end apart: 13 -> 12, of which waited for: 7 -> 6; matrix products, arithmetic and copies ran while one was open for 51% -> 57% of each run, Pallas kernels for 0% -> 0%
where the time goes in v1:
time: 491 us; the launch traced here: 489 us
  other arithmetic  240 us (49%)
  matrix products  87.3 us (18%)
  local copies, waits for them, and re-layouts  66.8 us (14%)
  starting transfers between devices  36.5 us (7%)
  blocking collectives  34.6 us (7%)
  waiting for transfers between devices  21.9 us (4%)
    another operation x1, other arithmetic  187 us
    dot_general x1, local copies, waits for them, and re-layouts, analyse(): lax.dot_general(table_now, flat_rows, (((0,), (1,)), ((), ())), preferred...  51.4 us
    dot_general x2, matrix products, analyse(): lax.dot_general(table_now, flat_rows, (((0,), (1,)), ((), ())), preferred...  39 us
    dot_general x2, matrix products, synthesise(): lax.dot_general(scaled, table_now, (((0,), (1,)), ((), ())), preferred_el...  36.8 us
    dot_general x1, other arithmetic, analyse(): lax.dot_general(table_now, flat_rows, (((0,), (1,)), ((), ())), preferred...  29.5 us
    ppermute x10, starting transfers between devices, passed_along(): return lax.ppermute(value, axis, pairs)  25 us
    all_gather x2, blocking collectives, on_device(): lax.all_gather(partial_value.astype(jnp.bfloat16), 'deg')  15 us
    dot_general x2, matrix products, legendre(): jnp.einsum('cmfl,mil->cmfi', scaled, basis, preferred_element_type=jnp.fl...  11.5 us
  transfers between devices with their start and end apart: 12, of which 6 were waited for; matrix products, arithmetic and copies ran while one was open for 57% of the time, Pallas kernels for 0%

profile of v1, /device:TPU:0, one launch (start us, length us, event | category | flops | bytes accessed | tf_op | source)
XLA Modules:
  0.0 488.7 jit_solution(7443802094811250249)
XLA Ops:
  7.9 187.3 %sine_convert_fusion = (bf16[10752,1024]{1,0:T(8,128)(2,1)}, bf16[10752,1024]{1,0:T(8,128)(2,1)}) fusion(), kind=kLoop, calls=%fused_computation.8 | loop fusion | flops 121110528 | bytes 44040192 | tf_op jit(solution)/shard_map/convert.21
  196.0 29.5 %fusion.9 = bf16[2048,10752]{0,1:T(8,128)(2,1)} fusion(bf16[10752,1024]{1,0:T(8,128)(2,1)} %get-tuple-element.48, bf16[10752,1024]{1,0:T(8,128)(2,1)} %get-tuple-element.49), kind=kLoop, calls=%fused_computation.14 | loop fusion | flops 88080384 | bytes 88080384 | tf_op jit(solution)/shard_map/dot_general | solution.py:36
  226.3 2.4 broadcast_multiply_fusion.1
  228.7 6.7 %collective-permute-start.3 = (bf16[1,10752]{1,0:T(2,128)(2,1)S(1)}, bf16[1,10752]{1,0:T(2,128)(2,1)S(1)}, u32[]{:S(2)}, u32[]{:S(2)}) collective-permute-start(bf16[1,10752]{1,0:T(2,128)(2,1)S(1)} %slice.279), channel_id=1, source_target_pairs={{0,4},{4,8},{8,12},{12,16},{16,20},{20,24},{24,28},{1,5},{5,9},{9,... | collective-permute-start | bytes 64520 | tf_op jit(solution)/shard_map/ppermute | solution.py:18
  235.5 51.4 %copy.28 = bf16[2048,10752]{1,0:T(8,128)(2,1)} copy(bf16[2048,10752]{0,1:T(8,128)(2,1)} %fusion.9) | data formatting | bytes 88080384 | tf_op jit(solution)/shard_map/dot_general | solution.py:36
  287.9 19.5 %fusion.66 = bf16[2,1024,2,8]{1,3,2,0:T(8,128)(2,1)S(1)} fusion(bf16[2,1024,10752,1]{2,1,3,0:T(8,128)(2,1)} %bitcast.190, bf16[1,8,10752]{2,1,0:T(8,128)(2,1)S(1)} %get-tuple-element.22, bf16[1,8,10752]{2,1,0:T(8,128)(2,1)S(1)} %copy-done.11, f32[2,8]{1,0:T(2,128)S(1)} %get-tuple-element.46), kind=kOutput, calls=%fused_computation.37 | convolution fusion | flops 705396736 | bytes 44449856 | tf_op jit(solution)/shard_map/dot_general | solution.py:36
  308.1 1.7 reshape.81
  309.8 8.1 %all-to-all-start = ((bf16[8,2,2048]{2,1,0:T(2,128)(2,1)}), bf16[8,2,2048]{2,1,0:T(2,128)(2,1)S(1)}, u32[]{:S(2)}, u32[]{:S(2)}) async-start(bf16[8,2,2048]{2,1,0:T(2,128)(2,1)} %reshape.81), calls=%async_computation | async-start | bytes 131072 | tf_op jit(solution)/shard_map/all_to_all | solution.py:110
  317.9 6.9 %all-to-all-done = bf16[8,2,2048]{2,1,0:T(2,128)(2,1)S(1)} async-done(((bf16[8,2,2048]{2,1,0:T(2,128)(2,1)}), bf16[8,2,2048]{2,1,0:T(2,128)(2,1)S(1)}, u32[]{:S(2)}, u32[]{:S(2)}) %all-to-all-start) | async-done | bytes 65568 | tf_op jit(solution)/shard_map/all_to_all | solution.py:110
  327.5 5.4 %fusion.61 = bf16[2,128,2,64]{3,2,0,1:T(2,128)(2,1)S(1)} fusion(bf16[128,64,256]{2,1,0:T(8,128)(2,1)} %param.16, bf16[2,128,2,64]{3,2,0,1:T(2,128)(2,1)S(1)} %copy.32, f32[256]{0:T(256)S(1)} %copy-done.12), kind=kOutput, calls=%fused_computation.34 | convolution fusion | flops 33849344 | bytes 4326400 | tf_op jit(solution)/shard_map/cmfl,mil->cmfi/dot_general | solution.py:46
  332.9 7.3 %all-gather = bf16[8,128,2,64]{3,2,0,1:T(2,128)(2,1)S(1)} all-gather(bf16[2,128,2,64]{3,2,0,1:T(2,128)(2,1)S(1)} %fusion.61), channel_id=2, replica_groups=mesh['lat'=8,'deg'=4] {'deg'}, dimensions={0}, use_global_device_ids=true | all-gather | bytes 327680 | tf_op jit(solution)/shard_map/all_gather | solution.py:112
  342.1 3.4 all-to-all-start.1
  345.5 6.8 %all-to-all-done.1 = bf16[2,128,2,64]{1,0,2,3:T(2,128)(2,1)S(1)} async-done(((bf16[2,128,2,64]{1,0,2,3:T(2,128)(2,1)}), bf16[2,128,2,64]{1,0,2,3:T(2,128)(2,1)S(1)}, u32[]{:S(2)}, u32[]{:S(2)}) %all-to-all-start.1) | async-done | bytes 65568 | tf_op jit(solution)/shard_map/all_to_all | solution.py:113
  352.4 18.4 %fusion.10 = f32[2,8,10752]{2,1,0:T(8,128)} fusion(bf16[10752,1024]{1,0:T(8,128)(2,1)} %get-tuple-element.48, bf16[10752,1024]{1,0:T(8,128)(2,1)} %get-tuple-element.49, f32[2,8]{1,0:T(2,128)S(1)} %get-tuple-element.47, bf16[2048,16]{0,1:T(8,128)(2,1)S(1)} %all_to_all.59, bf16[2048]{0:T(1024)(128)(2,1)S(1)} %bitcast.214), kind=kOutput, calls=%fused_computation.15 | convolution fusion | flops 792928256 | bytes 44798016 | tf_op jit(solution)/shard_map/dot_general | solution.py:53
  375.1 3.3 collective-permute-done.4
  378.4 1.6 collective-permute-done.6
  380.1 2.4 fusion.139
  382.6 4.8 collective-permute-start.5
  387.5 2.5 collective-permute-start.7
  390.5 1.8 multiply_bitcast_fusion.1
  392.8 19.5 %fusion.67 = bf16[2,1024,2,8]{1,3,2,0:T(8,128)(2,1)S(1)} fusion(bf16[2,1024,10752,1]{2,1,3,0:T(8,128)(2,1)} %bitcast.191, bf16[1,8,10752]{2,1,0:T(8,128)(2,1)S(1)} %get-tuple-element.14, bf16[1,8,10752]{2,1,0:T(8,128)(2,1)S(1)} %get-tuple-element.12, f32[2,8]{1,0:T(2,128)S(1)} %get-tuple-element.46), kind=kOutput, calls=%fused_computation.38 | convolution fusion | flops 705396736 | bytes 44449856 | tf_op jit(solution)/shard_map/dot_general | solution.py:36
  414.1 10.3 %all_to_all.72 = bf16[8,2,2048]{2,1,0:T(2,128)(2,1)S(1)} all-to-all(bf16[8,2,2048]{2,1,0:T(2,128)(2,1)S(1)} %reshape.83), channel_id=1, replica_groups=mesh['lat'=8,'deg'=4] {'lat'}, dimensions={0} | all-to-all | bytes 131072 | tf_op jit(solution)/shard_map/all_to_all | solution.py:110
  427.7 6.1 %fusion.56 = bf16[2,128,2,64]{3,2,0,1:T(2,128)(2,1)} fusion(bf16[128,64,256]{2,1,0:T(8,128)(2,1)} %param.16, bf16[2,128,2,64]{3,2,0,1:T(2,128)(2,1)} %copy.38, f32[256]{0:T(256)S(1)} %copy-done.12), kind=kOutput, calls=%fused_computation.33 | convolution fusion | flops 33849344 | bytes 4326400 | tf_op jit(solution)/shard_map/cmfl,mil->cmfi/dot_general | solution.py:46
  433.8 7.7 %all-gather.1 = bf16[8,128,2,64]{3,2,0,1:T(2,128)(2,1)} all-gather(bf16[2,128,2,64]{3,2,0,1:T(2,128)(2,1)} %fusion.56), channel_id=3, replica_groups=mesh['lat'=8,'deg'=4] {'deg'}, dimensions={0}, use_global_device_ids=true | all-gather | bytes 327680 | tf_op jit(solution)/shard_map/all_gather | solution.py:112
  441.5 2.6 reduce_sum.25
  445.1 9.3 %all_to_all.73 = bf16[2,128,2,64]{1,0,2,3:T(2,128)(2,1)S(1)} all-to-all(bf16[2,128,2,64]{1,0,2,3:T(2,128)(2,1)S(1)} %copy.39), channel_id=1, replica_groups=mesh['lat'=8,'deg'=4] {'lat'}, dimensions={3} | all-to-all | bytes 131072 | tf_op jit(solution)/shard_map/all_to_all | solution.py:113
  455.1 18.4 %fusion.13 = f32[2,8,10752]{2,1,0:T(8,128)} fusion(bf16[10752,1024]{1,0:T(8,128)(2,1)} %get-tuple-element.48, bf16[10752,1024]{1,0:T(8,128)(2,1)} %get-tuple-element.49, f32[2,8]{1,0:T(2,128)S(1)} %get-tuple-element.47, bf16[2048,16]{0,1:T(8,128)(2,1)} %all_to_all.67, bf16[2048]{0:T(1024)(128)(2,1)S(1)} %bitcast.215), kind=kOutput, calls=%fused_computation.16 | convolution fusion | flops 792928256 | bytes 44798016 | tf_op jit(solution)/shard_map/dot_general | solution.py:53
  473.5 1.9 fusion.68
  476.7 1.9 pad_maximum_fusion.4
  478.8 2.5 collective-permute-done.8
  481.4 1.4 fusion.130
  482.8 3.2 collective-permute-start.9
  (114 shorter events, 31.4 us)
Async XLA Ops:
  0.6 194.6 %copy-start.2 = (f32[8,10752]{1,0:T(8,128)S(1)}, f32[8,10752]{1,0:T(8,128)}, u32[]{:S(2)}) copy-start(f32[8,10752]{1,0:T(8,128)} %param.9) | copy-start | bytes 1032196
  2.0 224.2 %collective-permute-start.2 = (bf16[1,10752]{1,0:T(2,128)(2,1)S(1)}, bf16[1,10752]{1,0:T(2,128)(2,1)S(1)}, u32[]{:S(2)}, u32[]{:S(2)}) collective-permute-start(bf16[1,10752]{1,0:T(2,128)(2,1)S(1)} %slice.280), channel_id=1, source_target_pairs={{4,0},{8,4},{12,8},{16,12},{20,16},{24,20},{28,24},{5,1},{9,5},{13... | collective-permute-start | bytes 64520 | tf_op jit(solution)/shard_map/ppermute | solution.py:18
  4.3 221.9 %collective-permute-start.1 = (bf16[1,10752]{1,0:T(2,128)(2,1)S(1)}, bf16[1,10752]{1,0:T(2,128)(2,1)S(1)}, u32[]{:S(2)}, u32[]{:S(2)}) collective-permute-start(bf16[1,10752]{1,0:T(2,128)(2,1)S(1)} %slice.281), channel_id=1, source_target_pairs={{4,0},{8,4},{12,8},{16,12},{20,16},{24,20},{28,24},{5,1},{9,5},{13... | collective-permute-start | bytes 64520 | tf_op jit(solution)/shard_map/ppermute | solution.py:18
  6.6 219.7 %collective-permute-start = (bf16[1,10752]{1,0:T(2,128)(2,1)S(1)}, bf16[1,10752]{1,0:T(2,128)(2,1)S(1)}, u32[]{:S(2)}, u32[]{:S(2)}) collective-permute-start(bf16[1,10752]{1,0:T(2,128)(2,1)S(1)} %slice.282), channel_id=1, source_target_pairs={{4,0},{8,4},{12,8},{16,12},{20,16},{24,20},{28,24},{5,1},{9,5},{13... | collective-permute-start | bytes 64520 | tf_op jit(solution)/shard_map/ppermute | solution.py:18
  195.9 29.9 %copy-start.1 = (f32[8,10752]{1,0:T(8,128)S(1)}, f32[8,10752]{1,0:T(8,128)}, u32[]{:S(2)}) copy-start(f32[8,10752]{1,0:T(8,128)} %param.13) | copy-start | bytes 1032196
  195.9 30.4 %copy-start = (s32[8,10752]{1,0:T(8,128)S(1)}, s32[8,10752]{1,0:T(8,128)}, u32[]{:S(2)}) copy-start(s32[8,10752]{1,0:T(8,128)} %param.15) | copy-start | bytes 1032196
  195.9 30.4 %slice-start = ((f32[8,10752]{1,0:T(8,128)}), f32[8,1]{1,0:T(8,128)S(1)}, s32[]{:S(2)}) async-start(f32[8,10752]{1,0:T(8,128)} %param.13), calls=%async_computation.4 | async-start | bytes 8192 | tf_op jit(solution)/shard_map/jit(_roll_static)/slice | solution.py:87
  228.7 151.4 %copy-start.5 = (f32[8,10752]{1,0:T(8,128)}, f32[8,10752]{1,0:T(8,128)S(1)}, u32[]{:S(2)}) copy-start(f32[8,10752]{1,0:T(8,128)S(1)} %get-tuple-element.34) | copy-start | bytes 1032196
  228.7 58.2 %collective-permute-start.3 = (bf16[1,10752]{1,0:T(2,128)(2,1)S(1)}, bf16[1,10752]{1,0:T(2,128)(2,1)S(1)}, u32[]{:S(2)}, u32[]{:S(2)}) collective-permute-start(bf16[1,10752]{1,0:T(2,128)(2,1)S(1)} %slice.279), channel_id=1, source_target_pairs={{0,4},{4,8},{8,12},{12,16},{16,20},{20,24},{24,28},{1,5},{5,9},{9,... | collective-permute-start | bytes 64520 | tf_op jit(solution)/shard_map/ppermute | solution.py:18
  235.5 52.4 %copy-start.11 = (bf16[1,8,10752]{2,1,0:T(8,128)(2,1)S(1)}, bf16[1,8,10752]{2,1,0:T(8,128)(2,1)}, u32[]{:S(2)}) copy-start(bf16[1,8,10752]{2,1,0:T(8,128)(2,1)} %convert_bitcast_fusion.3) | copy-start | bytes 516100
  286.9 40.6 %copy-start.12 = (f32[256]{0:T(256)S(1)}, f32[256]{0:T(256)}, u32[]{:S(2)}) copy-start(f32[256]{0:T(256)} %param.17) | copy-start | bytes 3076
  309.8 15.0 %all-to-all-start = ((bf16[8,2,2048]{2,1,0:T(2,128)(2,1)}), bf16[8,2,2048]{2,1,0:T(2,128)(2,1)S(1)}, u32[]{:S(2)}, u32[]{:S(2)}) async-start(bf16[8,2,2048]{2,1,0:T(2,128)(2,1)} %reshape.81), calls=%async_computation | async-start | bytes 131072 | tf_op jit(solution)/shard_map/all_to_all | solution.py:110
  327.5 52.6 %copy-start.3 = (f32[8,10752]{1,0:T(8,128)S(1)}, f32[8,10752]{1,0:T(8,128)}, u32[]{:S(2)}) copy-start(f32[8,10752]{1,0:T(8,128)} %param.14) | copy-start | bytes 1032196
  327.5 52.6 %copy-start.7 = (f32[8,10752]{1,0:T(8,128)S(1)}, f32[8,10752]{1,0:T(8,128)}, u32[]{:S(2)}) copy-start(f32[8,10752]{1,0:T(8,128)} %get-tuple-element.35) | copy-start | bytes 1032196
  341.4 29.5 %copy-start.9 = (f32[8,10752]{1,0:T(8,128)S(1)}, f32[8,10752]{1,0:T(8,128)}, u32[]{:S(2)}) copy-start(f32[8,10752]{1,0:T(8,128)} %param.11) | copy-start | bytes 1032196
  342.1 10.2 %all-to-all-start.1 = ((bf16[2,128,2,64]{1,0,2,3:T(2,128)(2,1)}), bf16[2,128,2,64]{1,0,2,3:T(2,128)(2,1)S(1)}, u32[]{:S(2)}, u32[]{:S(2)}) async-start(bf16[2,128,2,64]{1,0,2,3:T(2,128)(2,1)} %copy.33), calls=%async_computation.1 | async-start | bytes 131072 | tf_op jit(solution)/shard_map/all_to_all | solution.py:113
  372.2 6.2 %collective-permute-start.4 = (bf16[1,10752]{1,0:T(2,128)(2,1)S(1)}, bf16[1,10752]{1,0:T(2,128)(2,1)S(1)}, u32[]{:S(2)}, u32[]{:S(2)}) collective-permute-start(bf16[1,10752]{1,0:T(2,128)(2,1)S(1)} %slice.278), channel_id=1, source_target_pairs={{4,0},{8,4},{12,8},{16,12},{20,16},{24,20},{28,24},{5,1},{9,5},{13... | collective-permute-start | bytes 64520 | tf_op jit(solution)/shard_map/ppermute | solution.py:18
  373.5 6.5 %collective-permute-start.6 = (bf16[1,10752]{1,0:T(2,128)(2,1)S(1)}, bf16[1,10752]{1,0:T(2,128)(2,1)S(1)}, u32[]{:S(2)}, u32[]{:S(2)}) collective-permute-start(bf16[1,10752]{1,0:T(2,128)(2,1)S(1)} %slice.276), channel_id=1, source_target_pairs={{4,0},{8,4},{12,8},{16,12},{20,16},{24,20},{28,24},{5,1},{9,5},{13... | collective-permute-start | bytes 64520 | tf_op jit(solution)/shard_map/ppermute | solution.py:18
  382.6 7.5 %collective-permute-start.5 = (bf16[1,10752]{1,0:T(2,128)(2,1)S(1)}, bf16[1,10752]{1,0:T(2,128)(2,1)S(1)}, u32[]{:S(2)}, u32[]{:S(2)}) collective-permute-start(bf16[1,10752]{1,0:T(2,128)(2,1)S(1)} %slice.277), channel_id=1, source_target_pairs={{0,4},{4,8},{8,12},{12,16},{16,20},{20,24},{24,28},{1,5},{5,9},{9,... | collective-permute-start | bytes 64520 | tf_op jit(solution)/shard_map/ppermute | solution.py:18
  387.5 5.0 %collective-permute-start.7 = (bf16[1,10752]{1,0:T(2,128)(2,1)S(1)}, bf16[1,10752]{1,0:T(2,128)(2,1)S(1)}, u32[]{:S(2)}, u32[]{:S(2)}) collective-permute-start(bf16[1,10752]{1,0:T(2,128)(2,1)S(1)} %slice.275), channel_id=1, source_target_pairs={{0,4},{4,8},{8,12},{12,16},{16,20},{20,24},{24,28},{1,5},{5,9},{9,... | collective-permute-start | bytes 64520 | tf_op jit(solution)/shard_map/ppermute | solution.py:18
  425.5 51.1 %copy-start.10 = (f32[1,8,10752]{2,1,0:T(8,128)S(1)}, f32[1,8,10752]{2,1,0:T(8,128)}, u32[]{:S(2)}) copy-start(f32[1,8,10752]{2,1,0:T(8,128)} %get-tuple-element.4) | copy-start | bytes 1032196
  427.6 53.7 %copy-start.4 = (f32[8,10752]{1,0:T(8,128)S(1)}, f32[8,10752]{1,0:T(8,128)}, u32[]{:S(2)}) copy-start(f32[8,10752]{1,0:T(8,128)} %param.14) | copy-start | bytes 1032196
  427.7 53.7 %copy-start.6 = (f32[8,10752]{1,0:T(8,128)S(1)}, f32[8,10752]{1,0:T(8,128)}, u32[]{:S(2)}) copy-start(f32[8,10752]{1,0:T(8,128)} %copy-done.5) | copy-start | bytes 1032196
  427.7 53.7 %copy-start.8 = (f32[8,10752]{1,0:T(8,128)S(1)}, f32[8,10752]{1,0:T(8,128)}, u32[]{:S(2)}) copy-start(f32[8,10752]{1,0:T(8,128)} %get-tuple-element.35) | copy-start | bytes 1032196
  475.4 5.9 %collective-permute-start.8 = (bf16[1,10752]{1,0:T(2,128)(2,1)S(1)}, bf16[1,10752]{1,0:T(2,128)(2,1)S(1)}, u32[]{:S(2)}, u32[]{:S(2)}) collective-permute-start(bf16[1,10752]{1,0:T(2,128)(2,1)S(1)} %slice.274), channel_id=1, source_target_pairs={{4,0},{8,4},{12,8},{16,12},{20,16},{24,20},{28,24},{5,1},{9,5},{13... | collective-permute-start | bytes 64520 | tf_op jit(solution)/shard_map/ppermute | solution.py:18
  482.8 4.9 collective-permute-start.9
